TPU v7x, 512 devices: a whole 4x4x16 slice. The times are simulated.
512 devices in a mesh: seq: 64 (over y, z), chan: 8 (over x, core).
Axes of the slice: x: 4, y: 4, z: 16, core: 2. Of those that a mesh axis runs over, the one named last changes fastest.
Arguments:
- x1: bfloat16 [8192, 4096], P('seq', 'chan'), may hold values from -6 to 6
- x2: bfloat16 [8192, 4096], P('seq', 'chan'), may hold values from -6 to 6
- value: bfloat16 [8192, 4096], P('seq', 'chan'), may hold values from -6 to 6
- out_grad: bfloat16 [8192, 4096], P('seq', 'chan'), may hold values from -6 to 6
- short_weight: float32 [3, 4096], P(None, 'chan'), may hold values from -3.5 to 3.5
- coef: float32 [64, 4096], P(None, 'chan'), may hold values from -0.75 to 0.75
- rate: float32 [64], replicated, may hold values from 0.2 to 273.06667, as said below
Outputs:
- layer_output: bfloat16 [8192, 4096], P('seq', 'chan')
- grad_x1: bfloat16 [8192, 4096], P('seq', 'chan')
- grad_value: bfloat16 [8192, 4096], P('seq', 'chan')
- grad_coef: float32 [64, 4096], P(None, 'chan')
- grad_rate: float32 [64], replicated
Inputs may be any that keep to these rules, and one draw needn't show every extreme that they name: `rate`: decay rates of the basis functions, per 8192 positions.
All inputs are finite; a program needn't handle non-finite values.
Results may differ from a plain program's by a relative error of at most 0.011.
Values may be sent and summed in bfloat16 or wider, within the bound.
No kernel may reach another device: no remote copies, remote signals or barrier semaphores. Data moves between devices by JAX's collectives and lax.ppermute only.
A program may use at most 64 MiB of HBM per device.

v0:
```python
import math
import jax
import jax.numpy as jnp
from jax import lax
from jax.sharding import PartitionSpec as P

highest = lax.Precision.HIGHEST


def from_behind(shard, axis, by):
    peers = lax.axis_size(axis)
    pairs = [(i, i + by) for i in range(peers) if 0 <= i + by < peers]
    return lax.ppermute(shard, axis, pairs)


def angles(index, period):
    return 2.0 * math.pi / period * (index % period).astype(jnp.float32)


def basis_pair(rate, start, count, length):
    position = start + jnp.arange(count, dtype=jnp.int32)
    index = jnp.arange(rate.shape[0], dtype=jnp.int32)
    cycles = (index // 2 + 1) * (index // 2 + 1)
    turned = position[:, None] * cycles[None, :] % length
    angle = 2.0 * math.pi / length * turned.astype(jnp.float32)
    wave = jnp.where(index[None, :] % 2 == 0, jnp.cos(angle), jnp.sin(angle))
    scaled = position.astype(jnp.float32)[:, None] / length
    envelope = jnp.sqrt(2.0 * rate / length)[None, :] * jnp.exp(-rate[None, :] * scaled)
    phi = envelope * wave
    psi = (0.5 / rate[None, :] - scaled) * phi
    return (phi, psi)


def row_tables(rows):
    every = jnp.arange(rows, dtype=jnp.int32)
    angle = angles(every[:, None] * every[None, :], rows)
    return (jnp.cos(angle), jnp.sin(angle))


def forward_transform(columns):
    shards = lax.axis_size("seq")
    place = lax.axis_index("seq")
    rows = columns.shape[0]
    slab = rows // shards
    width = columns.shape[1]
    received = lax.all_to_all(
        columns.reshape(shards, slab, width), "seq", split_axis=0, concat_axis=0, tiled=True
    )
    flat = received.reshape(shards, slab * width)
    freq_low = jnp.arange(2 * shards, dtype=jnp.int32)
    sources = jnp.arange(shards, dtype=jnp.int32)
    first = angles(freq_low[:, None] * sources[None, :], 2 * shards)
    real_a = jnp.dot(jnp.cos(first), flat, precision=highest).reshape(2 * shards, slab, width)
    imag_a = -jnp.dot(jnp.sin(first), flat, precision=highest).reshape(2 * shards, slab, width)
    local_rows = place * slab + jnp.arange(slab, dtype=jnp.int32)
    twist = angles(freq_low[:, None] * local_rows[None, :], 2 * shards * rows)
    cos_t = jnp.cos(twist)[:, :, None]
    sin_t = jnp.sin(twist)[:, :, None]
    real_b = real_a * cos_t + imag_a * sin_t
    imag_b = imag_a * cos_t - real_a * sin_t
    gathered = lax.all_to_all(
        jnp.stack([real_b, imag_b]), "seq", split_axis=1, concat_axis=2, tiled=True
    )
    cos_m, sin_m = row_tables(rows)
    real_x = jnp.einsum("fm,rmk->rfk", cos_m, gathered[0], precision=highest) + jnp.einsum(
        "fm,rmk->rfk", sin_m, gathered[1], precision=highest
    )
    imag_x = jnp.einsum("fm,rmk->rfk", cos_m, gathered[1], precision=highest) - jnp.einsum(
        "fm,rmk->rfk", sin_m, gathered[0], precision=highest
    )
    return (real_x, imag_x)


def inverse_transform(real_x, imag_x):
    shards = lax.axis_size("seq")
    place = lax.axis_index("seq")
    rows = real_x.shape[1]
    slab = rows // shards
    width = real_x.shape[2]
    total = 2 * shards * rows
    cos_m, sin_m = row_tables(rows)
    real_b = jnp.einsum("mf,rfk->rmk", cos_m, real_x, precision=highest) - jnp.einsum(
        "mf,rfk->rmk", sin_m, imag_x, precision=highest
    )
    imag_b = jnp.einsum("mf,rfk->rmk", cos_m, imag_x, precision=highest) + jnp.einsum(
        "mf,rfk->rmk", sin_m, real_x, precision=highest
    )
    freq_low = place * 2 + jnp.arange(2, dtype=jnp.int32)
    every = jnp.arange(rows, dtype=jnp.int32)
    twist = angles(freq_low[:, None] * every[None, :], total)
    cos_t = jnp.cos(twist)[:, :, None]
    sin_t = jnp.sin(twist)[:, :, None]
    real_c = real_b * cos_t - imag_b * sin_t
    imag_c = real_b * sin_t + imag_b * cos_t
    spread = lax.all_to_all(
        jnp.stack([real_c, imag_c]), "seq", split_axis=2, concat_axis=1, tiled=True
    )
    targets = jnp.arange(shards, dtype=jnp.int32)
    all_low = jnp.arange(2 * shards, dtype=jnp.int32)
    last = angles(targets[:, None] * all_low[None, :], 2 * shards)
    real_flat = spread[0].reshape(2 * shards, slab * width)
    imag_flat = spread[1].reshape(2 * shards, slab * width)
    signal = (
        jnp.dot(jnp.cos(last), real_flat, precision=highest)
        - jnp.dot(jnp.sin(last), imag_flat, precision=highest)
    ) / total
    returned = lax.all_to_all(
        signal.reshape(shards, slab, width), "seq", split_axis=0, concat_axis=1, tiled=True
    )
    return returned.reshape(rows, width)


def per_device(x1, x2, value, out_grad, short_weight, coef, rate):
    shards = lax.axis_size("seq")
    place = lax.axis_index("seq")
    rows = x1.shape[0]
    chans = x1.shape[1]
    length = rows * shards
    taps = short_weight.shape[0]
    prior = from_behind(value[rows - (taps - 1) :], "seq", 1)
    extended = jnp.concatenate([prior, value], axis=0).astype(jnp.float32)
    mixed = short_weight[0][None, :] * extended[taps - 1 : taps - 1 + rows]
    for shift_k in range(1, taps):
        mixed = (
            mixed
            + short_weight[shift_k][None, :]
            * extended[taps - 1 - shift_k : taps - 1 - shift_k + rows]
        )
    first = x1.astype(jnp.float32)
    second = x2.astype(jnp.float32)
    gated = (first * mixed).astype(jnp.bfloat16)
    grad_conv = (out_grad.astype(jnp.float32) * second).astype(jnp.bfloat16)
    phi, psi = basis_pair(rate, place * rows, rows, length)
    kernel = jnp.dot(phi, coef, precision=highest)
    columns = jnp.concatenate(
        [gated.astype(jnp.float32), grad_conv.astype(jnp.float32), kernel], axis=1
    )
    real_x, imag_x = forward_transform(columns)
    real_u, imag_u = (real_x[:, :, :chans], imag_x[:, :, :chans])
    real_d, imag_d = (real_x[:, :, chans : 2 * chans], imag_x[:, :, chans : 2 * chans])
    real_h, imag_h = (real_x[:, :, 2 * chans :], imag_x[:, :, 2 * chans :])
    real_z = real_u * real_h - imag_u * imag_h
    imag_z = real_u * imag_h + imag_u * real_h
    real_g = real_h * real_d + imag_h * imag_d
    imag_g = real_h * imag_d - imag_h * real_d
    real_f = real_u * real_d + imag_u * imag_d
    imag_f = real_u * imag_d - imag_u * real_d
    signals = inverse_transform(
        jnp.concatenate([real_z, real_g, real_f], axis=2),
        jnp.concatenate([imag_z, imag_g, imag_f], axis=2),
    )
    conv = signals[:, :chans]
    grad_gated = signals[:, chans : 2 * chans]
    grad_filter = signals[:, 2 * chans :]
    coef_part = jnp.dot(phi.T, grad_filter, precision=highest) * length ** (-0.5)
    rate_part = jnp.sum(psi * jnp.dot(grad_filter, coef.T, precision=highest), axis=0)
    grad_coef = lax.psum(coef_part, "seq")
    rate_sum = lax.psum(rate_part, ("seq", "chan"))
    grad_rate = rate_sum * (length * chans * lax.axis_size("chan")) ** (-0.5)
    out_y = (second * conv).astype(jnp.bfloat16)
    grad_x1 = (grad_gated * mixed).astype(jnp.bfloat16)
    grad_mixed = grad_gated * first
    later = from_behind(grad_mixed[: taps - 1], "seq", -1)
    tail = jnp.concatenate([grad_mixed, later], axis=0)
    back = short_weight[0][None, :] * tail[0:rows]
    for shift_k in range(1, taps):
        back = back + short_weight[shift_k][None, :] * tail[shift_k : shift_k + rows]
    grad_value = back.astype(jnp.bfloat16)
    return (out_y, grad_x1, grad_value, grad_coef, grad_rate)


def solution(mesh):
    return jax.shard_map(
        per_device,
        mesh=mesh,
        in_specs=(
            P("seq", "chan"),
            P("seq", "chan"),
            P("seq", "chan"),
            P("seq", "chan"),
            P(None, "chan"),
            P(None, "chan"),
            P(),
        ),
        out_specs=(P("seq", "chan"), P("seq", "chan"), P("seq", "chan"), P(None, "chan"), P()),
        check_vma=False,
    )
```

profile of v0, /device:TPU:2, one launch (start us, length us, event | category | flops | bytes accessed | tf_op | source)
XLA Modules:
  0.0 738.9 jit_solution(4605748889626512701)
XLA Ops:
  7.9 3.8 collective-permute-start
  18.1 18.9 %all-to-all-start = ((f32[64,2,1536]{2,1,0:T(2,128)}), f32[64,2,1536]{2,1,0:T(2,128)S(1)}, u32[]{:S(2)}, u32[]{:S(2)}) async-start(f32[64,2,1536]{2,1,0:T(2,128)} %reshape.196), calls=%async_computation | async-start | bytes 1572864 | tf_op jit(solution)/shard_map/all_to_all | solution.py:46
  37.6 40.5 %all-to-all-done = f32[64,2,1536]{2,1,0:T(2,128)S(1)} async-done(((f32[64,2,1536]{2,1,0:T(2,128)}), f32[64,2,1536]{2,1,0:T(2,128)S(1)}, u32[]{:S(2)}, u32[]{:S(2)}) %all-to-all-start) | async-done | bytes 786464 | tf_op jit(solution)/shard_map/all_to_all | solution.py:46
  79.7 1.9 add_bitcast_fusion.1
  81.8 4.1 copy.26
  85.8 7.1 all-to-all-start.1
  92.9 11.9 %all-reduce.2.cloned.1.call-start = ((), (), s32[]{:S(2)}) async-start(), calls=%async_computation.4 | async-start | bytes 262144 | tf_op jit(solution)/shard_map/psum | solution.py:157
  106.2 129.6 %all-to-all-done.1 = f32[2,128,2,1536]{3,2,0,1:T(2,128)S(1)} async-done(((f32[2,128,2,1536]{3,2,0,1:T(2,128)}), f32[2,128,2,1536]{3,2,0,1:T(2,128)S(1)}, u32[]{:S(2)}, u32[]{:S(2)}) %all-to-all-start.1) | async-done | bytes 3145760 | tf_op jit(solution)/shard_map/all_to_all | solution.py:61
  235.8 1.6 copy.56
  237.4 2.3 fusion.154
  240.4 2.8 fusion.37
  243.2 2.5 copy.29
  245.7 1.7 fusion.35
  247.4 1.7 fusion.1
  249.2 1.7 fusion.2
  251.3 1.7 fusion.5
  252.9 1.7 fusion.4
  254.6 1.7 convolution_add_fusion
  256.3 2.1 subtract_bitcast_fusion
  258.7 3.6 copy.32
  262.2 150.9 %all_to_all.44 = f32[2,2,128,1536]{3,1,0,2:T(2,128)S(1)} all-to-all(f32[2,2,128,1536]{3,1,0,2:T(2,128)} %copy.32), channel_id=1, replica_groups=mesh['seq'=64,'chan'=8] {'seq'}, dimensions={2} | all-to-all | bytes 6291456 | tf_op jit(solution)/shard_map/all_to_all | solution.py:95
  420.4 49.5 %all_to_all.45 = f32[64,2,1536]{2,1,0:T(2,128)S(1)} all-to-all(f32[64,2,1536]{2,1,0:T(2,128)S(1)} %reshape.198), channel_id=1, replica_groups=mesh['seq'=64,'chan'=8] {'seq'}, dimensions={0} | all-to-all | bytes 1572864 | tf_op jit(solution)/shard_map/all_to_all | solution.py:107
  474.3 101.9 %psum.15 = f32[64]{0:T(128)S(1)} all-reduce(f32[64]{0:T(128)S(1)} %fusion.3), channel_id=1, replica_groups=mesh['seq'=64,'chan'=8] {'seq','chan'}, use_global_device_ids=true, to_apply=%region_2.3 | all-reduce | flops 64 | bytes 512 | tf_op jit(solution)/shard_map/psum | solution.py:158
  577.5 152.6 %all-reduce.2.cloned.1.call-done = f32[64,512]{1,0:T(8,128)} async-done(((f32[64,512]{1,0:T(8,128)}), f32[64,512]{1,0:T(8,128)}) %all-reduce.2.cloned.1.call-update) | async-done | bytes 131088 | tf_op jit(solution)/shard_map/psum | solution.py:157
  (78 shorter events, 26.3 us)
Async XLA Ops:
  7.2 5.8 copy-start
  7.9 6.5 collective-permute-start
  11.8 4.9 copy-start.6
  11.8 4.9 copy-start.8
  11.8 4.9 copy-start.10
  11.8 4.9 copy-start.12
  13.0 3.7 copy-start.4
  18.1 60.0 %all-to-all-start = ((f32[64,2,1536]{2,1,0:T(2,128)}), f32[64,2,1536]{2,1,0:T(2,128)S(1)}, u32[]{:S(2)}, u32[]{:S(2)}) async-start(f32[64,2,1536]{2,1,0:T(2,128)} %reshape.196), calls=%async_computation | async-start | bytes 1572864 | tf_op jit(solution)/shard_map/all_to_all | solution.py:46
  36.9 0.5 copy-start.17
  85.8 150.0 %all-to-all-start.1 = ((f32[2,128,2,1536]{3,2,0,1:T(2,128)}), f32[2,128,2,1536]{3,2,0,1:T(2,128)S(1)}, u32[]{:S(2)}, u32[]{:S(2)}) async-start(f32[2,128,2,1536]{3,2,0,1:T(2,128)} %copy.26), calls=%async_computation.1 | async-start | bytes 6291456 | tf_op jit(solution)/shard_map/all_to_all | solution.py:61
  92.9 637.2 %all-reduce.2.cloned.1.call-start = ((), (), s32[]{:S(2)}) async-start(), calls=%async_computation.4 | async-start | bytes 262144 | tf_op jit(solution)/shard_map/psum | solution.py:157
  245.7 1.7 copy-start.1
  254.6 1.7 copy-start.14
  254.6 1.7 copy-start.15
  420.3 50.2 %copy-start.5 = (f32[64]{0:T(128)S(1)}, f32[64]{0:T(128)}, u32[]{:S(2)}) copy-start(f32[64]{0:T(128)} %copy-done.4) | copy-start | bytes 772
  420.4 50.2 %copy-start.7 = (f32[128]{0:T(128)S(1)}, f32[128]{0:T(128)}, u32[]{:S(2)}) copy-start(f32[128]{0:T(128)} %copy-done.6) | copy-start | bytes 1540
  420.4 50.2 %copy-start.9 = (s32[128]{0:T(128)S(1)}, s32[128]{0:T(128)}, u32[]{:S(2)}) copy-start(s32[128]{0:T(128)} %copy-done.8) | copy-start | bytes 1540
  420.4 50.2 %copy-start.11 = (pred[64]{0:T(512)(128)(4,1)S(1)}, pred[64]{0:T(512)(128)(4,1)}, u32[]{:S(2)}) copy-start(pred[64]{0:T(512)(128)(4,1)} %copy-done.10) | copy-start | bytes 196
  420.4 50.2 %copy-start.13 = (s32[64]{0:T(128)S(1)}, s32[64]{0:T(128)}, u32[]{:S(2)}) copy-start(s32[64]{0:T(128)} %copy-done.12) | copy-start | bytes 772
  420.4 51.3 %copy-start.2 = (bf16[128,512]{1,0:T(8,128)(2,1)S(1)}, bf16[128,512]{1,0:T(8,128)(2,1)}, u32[]{:S(2)}) copy-start(bf16[128,512]{1,0:T(8,128)(2,1)} %param.7) | copy-start | bytes 393220
  420.4 51.3 %copy-start.3 = (bf16[128,512]{1,0:T(8,128)(2,1)S(1)}, bf16[128,512]{1,0:T(8,128)(2,1)}, u32[]{:S(2)}) copy-start(bf16[128,512]{1,0:T(8,128)(2,1)} %param.8) | copy-start | bytes 393220
  469.9 3.9 copy-start.16
  472.5 104.3 %collective-permute-start.1 = (f32[2,512]{1,0:T(2,128)S(1)}, f32[2,512]{1,0:T(2,128)S(1)}, u32[]{:S(2)}, u32[]{:S(2)}) collective-permute-start(f32[2,512]{1,0:T(2,128)S(1)} %slice.116), channel_id=1, source_target_pairs={{8,0},{16,8},{24,16},{32,24},{40,32},{48,40},{56,48},{64,56},{72,6... | collective-permute-start | bytes 12296 | tf_op jit(solution)/shard_map/ppermute | solution.py:13
Sparse Core Ops, SparseCore 0:
  473.9 256.1 all-reduce.1
where the time goes:
time: 746 us; the launch traced here: 739 us
  waiting for transfers between devices  323 us (43%)
  blocking collectives  302 us (40%)
  starting transfers between devices  42.9 us (6%)
  local copies, waits for them, and re-layouts  25.4 us (3%)
  matrix products  22.9 us (3%)
  between operations  15 us (2%)
  other arithmetic  7.67 us (1%)
    psum x1, waiting for transfers between devices, per_device(): grad_coef = lax.psum(coef_part, 'seq')  153 us
    all_to_all x1, blocking collectives, inverse_transform(): lax.all_to_all(jnp.stack([real_c, imag_c]), 'seq', split_axis=2, concat_a...  151 us
    all_to_all x1, waiting for transfers between devices, forward_transform(): lax.all_to_all(jnp.stack([real_b, imag_b]), 'seq', split_axis=1, concat_a...  130 us
    psum x1, blocking collectives, per_device(): rate_sum = lax.psum(rate_part, ('seq', 'chan'))  102 us
    all_to_all x1, blocking collectives, inverse_transform(): lax.all_to_all(signal.reshape(shards, slab, width), 'seq', split_axis=0,...  49.5 us
    all_to_all x1, waiting for transfers between devices, forward_transform(): lax.all_to_all(columns.reshape(shards, slab, width), 'seq', split_axis=0,...  40.5 us
    all_to_all x1, starting transfers between devices, forward_transform(): lax.all_to_all(columns.reshape(shards, slab, width), 'seq', split_axis=0,...  18.9 us
  transfers between devices with their start and end apart: 5, of which 3 were waited for; matrix products, arithmetic and copies ran while one was open for 1% of the time, Pallas kernels for 0%

commit v1 on v0

--- a/solution.py
+++ b/solution.py
@@ -155,7 +155,8 @@
     coef_part = jnp.dot(phi.T, grad_filter, precision=highest) * length ** (-0.5)
     rate_part = jnp.sum(psi * jnp.dot(grad_filter, coef.T, precision=highest), axis=0)
     grad_coef = lax.psum(coef_part, "seq")
-    rate_sum = lax.psum(rate_part, ("seq", "chan"))
+    parts = lax.all_gather(rate_part, ("seq", "chan"), axis=0, tiled=False)
+    rate_sum = parts.sum(axis=0)
     grad_rate = rate_sum * (length * chans * lax.axis_size("chan")) ** (-0.5)
     out_y = (second * conv).astype(jnp.bfloat16)
     grad_x1 = (grad_gated * mixed).astype(jnp.bfloat16)

time: 746 us -> 1200 us (1.61)
  waiting for transfers between devices: 323 us -> 921 us
  blocking collectives: 302 us -> 151 us
    unnamed x1 -> x3, waiting for transfers between devices: 0.02 us -> 439 us
    psum x1, waiting for transfers between devices: 153 us -> 255 us  [per_device(): grad_coef = lax.psum(coef_part, 'seq')]
    psum x1 -> x0, blocking collectives: 102 us -> none  [per_device(): rate_sum = lax.psum(rate_part, ('seq', 'chan'))]
    all_to_all x1 -> x0, blocking collectives: 49.5 us -> none  [inverse_transform(): lax.all_to_all(signal.reshape(shards, slab, width), 'seq', split_axis=0,...]
    all_to_all x0 -> x1, waiting for transfers between devices: none -> 42.8 us  [inverse_transform(): lax.all_to_all(signal.reshape(shards, slab, width), 'seq', split_axis=0,...]
  transfers between devices with their start and end apart: 5 -> 7, of which waited for: 3 -> 6; matrix products, arithmetic and copies ran while one was open for 1% -> 1% of each run, Pallas kernels for 0% -> 0%
where the time goes in v1:
time: 1200 us; the launch traced here: 1190 us
  waiting for transfers between devices  921 us (77%)
  blocking collectives  151 us (13%)
  starting transfers between devices  49.7 us (4%)
  local copies, waits for them, and re-layouts  27.7 us (2%)
  matrix products  22.9 us (2%)
  between operations  15 us (1%)
    unnamed x3, waiting for transfers between devices  439 us
    psum x1, waiting for transfers between devices, per_device(): grad_coef = lax.psum(coef_part, 'seq')  255 us
    all_to_all x1, blocking collectives, inverse_transform(): lax.all_to_all(jnp.stack([real_c, imag_c]), 'seq', split_axis=2, concat_a...  151 us
    all_to_all x1, waiting for transfers between devices, forward_transform(): lax.all_to_all(jnp.stack([real_b, imag_b]), 'seq', split_axis=1, concat_a...  141 us
    all_to_all x1, waiting for transfers between devices, inverse_transform(): lax.all_to_all(signal.reshape(shards, slab, width), 'seq', split_axis=0,...  42.8 us
    all_to_all x1, waiting for transfers between devices, forward_transform(): lax.all_to_all(columns.reshape(shards, slab, width), 'seq', split_axis=0,...  41 us
  transfers between devices with their start and end apart: 7, of which 6 were waited for; matrix products, arithmetic and copies ran while one was open for 1% of the time, Pallas kernels for 0%

profile of v1, /device:TPU:2, one launch (start us, length us, event | category | flops | bytes accessed | tf_op | source)
XLA Modules:
  0.0 1194.7 jit_solution(2344057409374398228)
XLA Ops:
  7.9 3.8 collective-permute-start
  18.1 18.9 %all-to-all-start = ((f32[64,2,1536]{2,1,0:T(2,128)}), f32[64,2,1536]{2,1,0:T(2,128)S(1)}, u32[]{:S(2)}, u32[]{:S(2)}) async-start(f32[64,2,1536]{2,1,0:T(2,128)} %reshape.196), calls=%async_computation | async-start | bytes 1572864 | tf_op jit(solution)/shard_map/all_to_all | solution.py:46
  37.1 41.0 %all-to-all-done = f32[64,2,1536]{2,1,0:T(2,128)S(1)} async-done(((f32[64,2,1536]{2,1,0:T(2,128)}), f32[64,2,1536]{2,1,0:T(2,128)S(1)}, u32[]{:S(2)}, u32[]{:S(2)}) %all-to-all-start) | async-done | bytes 786464 | tf_op jit(solution)/shard_map/all_to_all | solution.py:46
  79.7 1.9 add_bitcast_fusion.1
  81.8 4.1 copy.26
  85.8 18.9 %all-to-all-start.1 = ((f32[2,128,2,1536]{3,2,0,1:T(2,128)}), f32[2,128,2,1536]{3,2,0,1:T(2,128)S(1)}, u32[]{:S(2)}, u32[]{:S(2)}) async-start(f32[2,128,2,1536]{3,2,0,1:T(2,128)} %copy.26), calls=%async_computation.1 | async-start | bytes 6291456 | tf_op jit(solution)/shard_map/all_to_all | solution.py:61
  106.1 141.3 %all-to-all-done.1 = f32[2,128,2,1536]{3,2,0,1:T(2,128)S(1)} async-done(((f32[2,128,2,1536]{3,2,0,1:T(2,128)}), f32[2,128,2,1536]{3,2,0,1:T(2,128)S(1)}, u32[]{:S(2)}, u32[]{:S(2)}) %all-to-all-start.1) | async-done | bytes 3145760 | tf_op jit(solution)/shard_map/all_to_all | solution.py:61
  247.4 1.6 copy.56
  249.0 2.3 fusion.154
  252.0 2.8 fusion.37
  254.8 2.5 copy.29
  257.3 1.7 fusion.35
  259.0 1.7 fusion.1
  260.8 1.7 fusion.2
  262.9 1.7 fusion.5
  264.6 1.7 fusion.4
  266.3 1.7 convolution_add_fusion
  268.0 2.1 subtract_bitcast_fusion
  270.4 3.6 copy.32
  273.9 150.9 %all_to_all.44 = f32[2,2,128,1536]{3,1,0,2:T(2,128)S(1)} all-to-all(f32[2,2,128,1536]{3,1,0,2:T(2,128)} %copy.32), channel_id=1, replica_groups=mesh['seq'=64,'chan'=8] {'seq'}, dimensions={2} | all-to-all | bytes 6291456 | tf_op jit(solution)/shard_map/all_to_all | solution.py:95
  433.0 6.8 all-to-all-start.3
  439.9 42.8 %all-to-all-done.3 = f32[64,2,1536]{2,1,0:T(2,128)S(1)} async-done(((f32[64,2,1536]{2,1,0:T(2,128)}), f32[64,2,1536]{2,1,0:T(2,128)S(1)}, u32[]{:S(2)}, u32[]{:S(2)}) %all-to-all-start.3) | async-done | bytes 786464 | tf_op jit(solution)/shard_map/all_to_all | solution.py:107
  490.3 438.7 %all-reduce.6.cloned.1.call-done = f32[32768]{0:T(1024)} async-done(((f32[32768]{0:T(1024)}), f32[32768]{0:T(1024)}) %all-reduce.6.cloned.1.call-update) | async-done | bytes 131088
  930.6 255.3 %all-reduce.4.cloned.1.call-done = f32[64,512]{1,0:T(8,128)} async-done(((f32[64,512]{1,0:T(8,128)}), f32[64,512]{1,0:T(8,128)}) %all-reduce.4.cloned.1.call-update) | async-done | bytes 131088 | tf_op jit(solution)/shard_map/psum | solution.py:157
  (87 shorter events, 30.3 us)
Async XLA Ops:
  7.2 5.8 copy-start
  7.9 6.5 collective-permute-start
  11.8 3.7 copy-start.7
  11.8 3.6 copy-start.9
  11.8 3.6 copy-start.11
  11.8 3.6 copy-start.13
  13.0 2.4 copy-start.5
  18.1 60.0 %all-to-all-start = ((f32[64,2,1536]{2,1,0:T(2,128)}), f32[64,2,1536]{2,1,0:T(2,128)S(1)}, u32[]{:S(2)}, u32[]{:S(2)}) async-start(f32[64,2,1536]{2,1,0:T(2,128)} %reshape.196), calls=%async_computation | async-start | bytes 1572864 | tf_op jit(solution)/shard_map/all_to_all | solution.py:46
  36.9 44.6 %copy-start.18 = (s32[2]{0:T(128)}, s32[2]{0:T(128)S(1)}, u32[]{:S(2)}) copy-start(s32[2]{0:T(128)S(1)} %iota_add_fusion) | copy-start | bytes 28
  85.8 161.6 %all-to-all-start.1 = ((f32[2,128,2,1536]{3,2,0,1:T(2,128)}), f32[2,128,2,1536]{3,2,0,1:T(2,128)S(1)}, u32[]{:S(2)}, u32[]{:S(2)}) async-start(f32[2,128,2,1536]{3,2,0,1:T(2,128)} %copy.26), calls=%async_computation.1 | async-start | bytes 6291456 | tf_op jit(solution)/shard_map/all_to_all | solution.py:61
  266.3 1.8 copy-start.15
  266.3 1.8 copy-start.16
  433.0 50.3 %copy-start.2 = (bf16[128,512]{1,0:T(8,128)(2,1)S(1)}, bf16[128,512]{1,0:T(8,128)(2,1)}, u32[]{:S(2)}) copy-start(bf16[128,512]{1,0:T(8,128)(2,1)} %param.7) | copy-start | bytes 393220
  433.0 50.3 %copy-start.3 = (bf16[128,512]{1,0:T(8,128)(2,1)S(1)}, bf16[128,512]{1,0:T(8,128)(2,1)}, u32[]{:S(2)}) copy-start(bf16[128,512]{1,0:T(8,128)(2,1)} %param.8) | copy-start | bytes 393220
  433.0 49.7 %all-to-all-start.3 = ((f32[64,2,1536]{2,1,0:T(2,128)}), f32[64,2,1536]{2,1,0:T(2,128)S(1)}, u32[]{:S(2)}, u32[]{:S(2)}) async-start(f32[64,2,1536]{2,1,0:T(2,128)} %reshape.198), calls=%async_computation.3 | async-start | bytes 1572864 | tf_op jit(solution)/shard_map/all_to_all | solution.py:107
  439.8 489.2 %all-reduce.6.cloned.1.call-start = ((), (), s32[]{:S(2)}) async-start(), calls=%async_computation.5 | async-start | bytes 262144
  439.8 45.6 %copy-start.6 = (f32[64]{0:T(128)S(1)}, f32[64]{0:T(128)}, u32[]{:S(2)}) copy-start(f32[64]{0:T(128)} %copy-done.5) | copy-start | bytes 772
  439.8 45.6 %copy-start.8 = (f32[128]{0:T(128)S(1)}, f32[128]{0:T(128)}, u32[]{:S(2)}) copy-start(f32[128]{0:T(128)} %copy-done.7) | copy-start | bytes 1540
  439.8 45.6 %copy-start.10 = (s32[128]{0:T(128)S(1)}, s32[128]{0:T(128)}, u32[]{:S(2)}) copy-start(s32[128]{0:T(128)} %copy-done.9) | copy-start | bytes 1540
  439.8 45.6 %copy-start.12 = (pred[64]{0:T(512)(128)(4,1)S(1)}, pred[64]{0:T(512)(128)(4,1)}, u32[]{:S(2)}) copy-start(pred[64]{0:T(512)(128)(4,1)} %copy-done.11) | copy-start | bytes 196
  439.9 45.6 %copy-start.14 = (s32[64]{0:T(128)S(1)}, s32[64]{0:T(128)}, u32[]{:S(2)}) copy-start(s32[64]{0:T(128)} %copy-done.13) | copy-start | bytes 772
  439.9 45.6 %copy-start.17 = (f32[64]{0:T(128)S(1)}, f32[64]{0:T(128)}, u32[]{:S(2)}) copy-start(f32[64]{0:T(128)} %get-tuple-element.27) | copy-start | bytes 772
  484.1 5.5 collective-permute-start.1
  486.9 699.0 %all-reduce.4.cloned.1.call-start = ((), (), s32[]{:S(2)}) async-start(), calls=%async_computation.4 | async-start | bytes 262144 | tf_op jit(solution)/shard_map/psum | solution.py:157
  (2 other events, 2.4 us)
Sparse Core Ops, SparseCore 0:
  487.0 441.9 all-reduce.5
  933.3 252.5 all-reduce.3
